TPU v7x, 32 devices: a whole 2x2x4 slice. The times are simulated.
32 devices in a mesh: row: 4 (over x, core), col: 8 (over z, y).
Axes of the slice: x: 2, y: 2, z: 4, core: 2. Of those that a mesh axis runs over, the one named last changes fastest.
Arguments:
- front_matrix: float32 [16384, 16384], P('row', 'col'), may hold values from -2.5 to 202.5, as said below
- child_schur: float32 [2, 8192, 8192], P(None, 'row', 'col'), may hold values from -1.25 to 1.25
- child_index: int32 [2, 128], replicated, may hold values from 0 to 255, as said below
- child_valid: int32 [2, 128], replicated, may hold values 0 or 1
Outputs:
- trailing: float32 [16384, 16384], P('row', 'col')
- panel_factor: float32 [16384, 512], P('row')
Inputs may be any that keep to these rules, and one draw needn't show every extreme that they name: `front_matrix`: off the logical diagonal the entries lie in -2.5 to 2.5, on it in 97.5 to 202.5. `child_index`: each child's 128 entries are distinct front blocks. Among the child blocks a that share a mod 4, exactly 8 land in front blocks of each value mod 4; among the child blocks b that share b mod 8, at most 2 land in front blocks of any one value mod 8, and some value takes exactly 2.
All inputs are finite; a program needn't handle non-finite values.
Results may differ from a plain program's by a relative error of at most 0.00005.
Values sent between devices are 32-bit elements; how exact they have to be, the bound alone decides.
A program may use at most 512 MiB of HBM per device.

v0:
```python
import jax
import jax.numpy as jnp
from jax import lax
from jax.sharding import PartitionSpec as P

CHILD = 8192
PANEL = 512
BLK = 64


exact_mode = lax.Precision.HIGHEST


def spread_2(shard, axis, root):
    mine = lax.axis_index(axis) == root
    return lax.psum(jnp.where(mine, shard, jnp.zeros_like(shard)), axis)


def take_rows(source, indices):
    return jnp.take(source, indices, axis=0)


def place_blocks(arrived, col_source, row_source):
    picked = jnp.take(arrived, col_source, axis=0)
    return jnp.take(picked, row_source, axis=1)


def on_device(front_matrix, child_schur, child_index, child_valid):
    row_count = lax.axis_size("row")
    col_count = lax.axis_size("col")
    row_place = lax.axis_index("row")
    col_place = lax.axis_index("col")
    local_rows, local_cols = front_matrix.shape
    row_blocks = local_rows // BLK
    col_blocks = local_cols // BLK
    child_blocks = CHILD // BLK
    child_rowblk = child_schur.shape[1] // BLK
    child_colblk = child_schur.shape[2] // BLK
    per_owner = child_blocks // (row_count * row_count)
    col_multi = max(1, child_blocks // (col_count * col_count))
    row_slots = row_count * per_owner
    col_slots = col_count * col_multi
    validity = child_valid.astype(jnp.float32)
    all_blocks = jnp.arange(child_blocks)
    owner_row = child_index % row_count
    owner_col = child_index % col_count
    sender_row = all_blocks % row_count
    sender_col = all_blocks % col_count
    before = all_blocks[None, :] < all_blocks[:, None]
    earlier_row = (sender_row[:, None] == sender_row[None, :]) & before
    earlier_col = (sender_col[:, None] == sender_col[None, :]) & before
    row_rank = jnp.sum(
        (earlier_row[None] & (owner_row[:, :, None] == owner_row[:, None, :])).astype(jnp.int32),
        axis=2,
    )
    col_rank = jnp.sum(
        (earlier_col[None] & (owner_col[:, :, None] == owner_col[:, None, :])).astype(jnp.int32),
        axis=2,
    )
    row_key = owner_row * per_owner + row_rank
    col_key = owner_col * col_multi + col_rank
    local_arow = row_place + row_count * jnp.arange(child_rowblk)
    mine_rowkey = jnp.take(row_key, local_arow, axis=1)
    row_hit_send = mine_rowkey[:, :, None] == jnp.arange(row_slots)[None, None, :]
    src_row = jnp.sum(
        row_hit_send.astype(jnp.int32) * jnp.arange(child_rowblk)[None, :, None], axis=1
    )
    local_bcol = col_place + col_count * jnp.arange(child_colblk)
    mine_colkey = jnp.take(col_key, local_bcol, axis=1)
    col_hit_send = mine_colkey[:, :, None] == jnp.arange(col_slots)[None, None, :]
    src_col = jnp.sum(
        col_hit_send.astype(jnp.int32) * jnp.arange(child_colblk)[None, :, None], axis=1
    )
    has_col = jnp.sum(col_hit_send.astype(jnp.float32), axis=1)
    blocks = child_schur.reshape(2, child_rowblk, BLK, child_colblk * BLK)
    outgoing = jax.vmap(take_rows)(blocks, src_row)
    outgoing = outgoing.reshape(2, row_slots * BLK, child_colblk * BLK)
    section_one = lax.all_to_all(outgoing, "row", split_axis=1, concat_axis=1, tiled=True)
    section_one = section_one.reshape(2, row_slots, BLK, child_colblk, BLK).transpose(0, 3, 1, 2, 4)
    onward = jax.vmap(take_rows)(section_one, src_col) * has_col[:, :, None, None, None]
    onward = onward.reshape(2, col_slots * row_slots, BLK * BLK)
    section_two = lax.all_to_all(onward, "col", split_axis=1, concat_axis=1, tiled=True)
    arrived = section_two.reshape(2, col_slots, row_slots, BLK, BLK)
    front_rowblk = row_place + row_count * jnp.arange(row_blocks)
    match_rows = (child_index[:, None, :] == front_rowblk[None, :, None]).astype(jnp.int32)
    row_slot_of = sender_row[None, :] * per_owner + row_rank
    row_source = jnp.sum(match_rows * row_slot_of[:, None, :], axis=2)
    row_weight = jnp.sum(match_rows.astype(jnp.float32) * validity[:, None, :], axis=2)
    front_colblk = col_place + col_count * jnp.arange(col_blocks)
    match_cols = (child_index[:, None, :] == front_colblk[None, :, None]).astype(jnp.int32)
    col_slot_of = sender_col[None, :] * col_multi + col_rank
    col_source = jnp.sum(match_cols * col_slot_of[:, None, :], axis=2)
    col_weight = jnp.sum(match_cols.astype(jnp.float32) * validity[:, None, :], axis=2)
    placed = jax.vmap(place_blocks)(arrived, col_source, row_source)
    placed = placed * col_weight[:, :, None, None, None] * row_weight[:, None, :, None, None]
    contributions = placed.transpose(0, 2, 3, 1, 4).reshape(2, local_rows, local_cols)
    extended = front_matrix + contributions[0] + contributions[1]
    panel_width = PANEL // BLK
    columns = []
    for root_index in range(panel_width):
        columns.append(spread_2(extended[:, :BLK], "col", root_index))
    panel_cols = jnp.concatenate(columns, axis=1)
    corner_rows = []
    for root_index in range(panel_width):
        start = root_index // row_count * BLK
        corner_rows.append(spread_2(panel_cols[start : start + BLK], "row", root_index % row_count))
    corner = jnp.concatenate(corner_rows, axis=0)
    lower_factor = jnp.linalg.cholesky(corner)
    solved = jax.scipy.linalg.solve_triangular(lower_factor, panel_cols.T, lower=True).T
    logical_blk = jnp.arange(row_blocks) * row_count + row_place
    factor_blocks = lower_factor.reshape(panel_width, BLK, PANEL)
    picked = jnp.take(factor_blocks, jnp.minimum(logical_blk, panel_width - 1), axis=0)
    in_panel = (logical_blk < panel_width)[:, None, None]
    panel_factor = jnp.where(in_panel, picked, solved.reshape(row_blocks, BLK, PANEL)).reshape(
        local_rows, PANEL
    )
    spread = col_count // row_count
    arranged = panel_factor.reshape(col_blocks, spread, BLK, PANEL)
    chosen = lax.dynamic_index_in_dim(arranged, col_place // row_count, axis=1, keepdims=False)
    chosen = chosen.reshape(col_blocks * BLK, PANEL)
    across = spread_2(chosen, "row", col_place % row_count)
    update = jnp.einsum("rp,cp->rc", panel_factor, across, precision=exact_mode)
    logical_row = jnp.arange(local_rows) // BLK * row_count + row_place
    logical_col = jnp.arange(local_cols) // BLK * col_count + col_place
    retained = (logical_row >= panel_width)[:, None] & (logical_col >= panel_width)[None, :]
    trailing = jnp.where(retained, extended - update, jnp.zeros_like(update))
    return (trailing, panel_factor)


def solution(mesh):
    in_specs = (P("row", "col"), P(None, "row", "col"), P(), P())
    out_specs = (P("row", "col"), P("row", None))
    return jax.shard_map(
        on_device, mesh=mesh, in_specs=in_specs, out_specs=out_specs, check_vma=False
    )
```

profile of v0, /device:TPU:0, one launch (start us, length us, event | category | flops | bytes accessed | tf_op | source)
XLA Modules:
  0.0 2514.7 jit_solution(158339150338002922)
XLA Ops:
  11.1 15.3 gather_fusion.3
  26.5 6.6 bitcast_select_fusion
  33.1 25.1 copy.167
  58.2 7.0 all-to-all-start
  66.7 182.2 %all-to-all-done = f32[2,2048,1024]{2,0,1:T(2,128)} async-done(((f32[2,2048,1024]{2,0,1:T(2,128)}), f32[2,2048,1024]{2,0,1:T(2,128)}, u32[]{:S(2)}, u32[]{:S(2)}) %all-to-all-start) | async-done | bytes 16777248 | tf_op jit(solution)/shard_map/all_to_all | solution.py:78
  248.9 30.4 %reshape.537 = f32[2,32,64,16,64]{4,3,0,2,1:T(8,128)} reshape(f32[2,2048,1024]{2,0,1:T(2,128)} %all-to-all-done) | data formatting | bytes 33554432 | tf_op jit(solution)/shard_map/reshape | solution.py:79
  279.3 27.6 %copy.189 = f32[2,32,64,16,64]{4,2,1,3,0:T(8,128)} copy(f32[2,32,64,16,64]{4,3,0,2,1:T(8,128)} %reshape.537) | data formatting | bytes 33554432 | tf_op jit(solution)/shard_map/reshape | solution.py:79
  306.9 23.0 gather_fusion.4
  329.9 27.9 %gather.44 = f32[2,512,4096]{2,1,0:T(8,128)} reshape(f32[32,32,64,64]{3,2,1,0:T(8,128)} %gather_fusion.4) | data formatting | bytes 33554432 | tf_op jit(solution)/shard_map/vmap(jit(_take))/gather | solution.py:20
  357.8 7.3 select_multiply_fusion
  365.1 18.9 copy.170
  384.0 6.8 all-to-all-start.1
  392.2 31.1 %copy.174 = f32[4096,2048]{0,1:T(8,128)} copy(f32[4096,2048]{1,0:T(8,128)} %param.4) | data formatting | bytes 67108864 | tf_op args[0]
  424.7 328.9 %all-to-all-done.1 = f32[2,512,4096]{2,0,1:T(2,128)} async-done(((f32[2,512,4096]{2,0,1:T(2,128)}), f32[2,512,4096]{2,0,1:T(2,128)}, u32[]{:S(2)}, u32[]{:S(2)}) %all-to-all-start.1) | async-done | bytes 16777248 | tf_op jit(solution)/shard_map/all_to_all | solution.py:82
  753.6 30.7 %reshape.465 = f32[2,16,32,64,64]{4,3,0,2,1:T(8,128)} reshape(f32[2,512,4096]{2,0,1:T(2,128)} %all-to-all-done.1) | data formatting | bytes 33554432 | tf_op jit(solution)/shard_map/reshape | solution.py:83
  784.4 40.0 %gather_fusion.5 = f32[64,32,64,64]{3,2,1,0:T(8,128)} fusion(f32[2,16,32,64,64]{4,3,0,2,1:T(8,128)} %reshape.465, s32[64]{0:T(128)S(1)} %reshape.523), kind=kCustom, calls=%fused_computation.5 | custom fusion | bytes 67109376 | tf_op jit(solution)/shard_map/vmap(jit(_take))/gather | solution.py:24
  824.3 44.6 %broadcast_select_fusion = f32[2,32,32,64,64]{4,3,2,1,0:T(8,128)} fusion(f32[2,32,32,64,64]{4,3,2,1,0:T(8,128)} %bitcast.10, pred[2,32]{1,0:T(4,128)(4,1)S(1)} %copy-done.12), kind=kLoop, calls=%fused_computation.13 | loop fusion | flops 8388608 | bytes 67108928 | tf_op jit(solution)/shard_map/vmap(jit(_take))/select_n | solution.py:24
  868.9 81.2 %gather_fusion.6 = f32[128,32,64,64]{3,2,1,0:T(8,128)} fusion(f32[2,32,32,64,64]{4,3,2,1,0:T(8,128)} %broadcast_select_fusion, s32[128]{0:T(128)S(1)} %reshape.529), kind=kCustom, calls=%fused_computation.6 | custom fusion | bytes 134218752 | tf_op jit(solution)/shard_map/vmap(jit(_take))/gather | solution.py:25
  950.1 190.8 %copy.187 = f32[2,64,32,64,64]{1,0,4,3,2:T(2,128)} copy(f32[2,64,32,64,64]{4,3,2,1,0:T(8,128)} %bitcast.12) | data formatting | bytes 134217728 | tf_op jit(solution)/shard_map/vmap(jit(_take))/gather | solution.py:25
  1140.9 88.2 %multiply_bitcast_fusion = f32[2,64,64,32,64]{1,0,4,2,3:T(2,128)} fusion(f32[2,64,32,64,64]{1,0,4,3,2:T(2,128)} %copy.187, pred[2,64]{1,0:T(4,128)(4,1)S(1)} %copy-done.14, f32[2,64]{1,0:T(2,128)S(1)} %copy-done.11, f32[2,32]{0,1:T(8,128)S(1)} %copy-done.9), kind=kLoop, calls=%fused_computation.9 | loop fusion | flops 50331648 | bytes 134218624 | tf_op jit(solution)/shard_map/mul | solution.py:95
  1229.1 143.6 %fusion.75 = (f32[1,64,64,32,64]{1,0,4,2,3:T(1,128)}, f32[1,64,64,32,64]{1,0,4,2,3:T(1,128)}) fusion(f32[2,64,64,32,64]{1,0,4,2,3:T(2,128)} %multiply_bitcast_fusion), kind=kLoop, calls=%fused_computation.218 | loop fusion | bytes 134217728 | tf_op jit(solution)/shard_map/slice | solution.py:97
  1372.7 134.8 %copy.173 = f32[1,64,64,32,64]{2,1,4,3,0:T(8,128)} copy(f32[1,64,64,32,64]{1,0,4,2,3:T(1,128)} %get-tuple-element.52) | data formatting | bytes 67108864 | tf_op jit(solution)/shard_map/slice | solution.py:97
  1507.5 54.7 %squeeze.8 = f32[4096,2048]{0,1:T(8,128)} reshape(f32[1,64,64,32,64]{2,1,4,3,0:T(8,128)} %copy.173) | data formatting | bytes 67108864 | tf_op jit(solution)/shard_map/squeeze | solution.py:97
  1562.2 134.8 %copy.175 = f32[1,64,64,32,64]{2,1,4,3,0:T(8,128)} copy(f32[1,64,64,32,64]{1,0,4,2,3:T(1,128)} %get-tuple-element.53) | data formatting | bytes 67108864 | tf_op jit(solution)/shard_map/slice | solution.py:97
  1697.0 54.7 %squeeze.9 = f32[4096,2048]{0,1:T(8,128)} reshape(f32[1,64,64,32,64]{2,1,4,3,0:T(8,128)} %copy.175) | data formatting | bytes 67108864 | tf_op jit(solution)/shard_map/squeeze | solution.py:97
  1751.7 43.8 %add_add_fusion = f32[4096,2048]{0,1:T(8,128)} fusion(f32[4096,2048]{0,1:T(8,128)} %squeeze.9, f32[4096,2048]{0,1:T(8,128)} %copy.174, f32[4096,2048]{0,1:T(8,128)} %squeeze.8), kind=kLoop, calls=%fused_computation.12 | loop fusion | flops 16777216 | bytes 134217728 | tf_op jit(solution)/shard_map/add | solution.py:97
  1795.5 4.6 slice_select_fusion
  1800.5 275.6 %all-reduce.9.cloned.1.call-done = (f32[4096,64]{0,1:T(8,128)}, f32[4096,64]{0,1:T(8,128)}, f32[4096,64]{0,1:T(8,128)}, f32[4096,64]{0,1:T(8,128)}, f32[4096,64]...) async-done(((f32[4096,64]{0,1:T(8,128)}, f32[4096,64]{0,1:T(8,128)}, f32[4096,64]{0,1:T(8,128)}, f32[4096,64]{0,1:T(8,128)}, ...) | async-done | bytes 8388624 | tf_op jit(solution)/shard_map/psum | solution.py:16
  2076.1 1.4 constant_dynamic-update-slice_fusion.7
  2077.6 1.4 constant_dynamic-update-slice_fusion.6
  2082.0 3.4 copy-done.3
  2085.4 1.4 slice_select_fusion.8
  2087.0 51.3 %all-reduce.11.cloned.1.call-done = (f32[64,512]{0,1:T(8,128)}, f32[64,512]{0,1:T(8,128)}, f32[64,512]{0,1:T(8,128)}, f32[64,512]{0,1:T(8,128)}, f32[64,512]{0,1...) async-done(((f32[64,512]{0,1:T(8,128)}, f32[64,512]{0,1:T(8,128)}, f32[64,512]{0,1:T(8,128)}, f32[64,512]{0,1:T(8,128)}, f32[64,512]{0,1:T(8,128)}, ...) | async-done | bytes 1048592 | tf_op jit(solution)/shard_map/psum | solution.py:16
  2138.3 2.3 concatenate.18
  2141.2 11.7 cholesky.104
  2153.1 9.8 custom-call.31
  2163.6 11.7 cholesky.217
  2176.7 10.0 custom-call.32
  2187.3 11.7 cholesky.238
  2199.7 9.8 custom-call.33
  2210.1 11.7 cholesky.255
  2225.6 10.6 while.1
  2226.3 2.0 bitcast_dynamic-update-slice_fusion.2
  2228.9 2.0 bitcast_dynamic-update-slice_fusion.2
  2231.5 2.0 bitcast_dynamic-update-slice_fusion.2
  2234.2 2.0 bitcast_dynamic-update-slice_fusion.2
  2236.1 40.2 %custom-call.34 = f32[4,128,128]{1,2,0:T(8,128)S(1)} custom-call(f32[4,128,128]{2,1,0:T(8,128)} %get-tuple-element.9), custom_call_target="InvertDiagBlocksLowerTriangular" | custom-call | tf_op jit(solution)/shard_map/jit(_solve_triangular)/triangular_solve | solution.py:109
  2276.3 3.5 fusion.13
  2279.8 3.6 convolution_subtract_fusion.1
  2283.4 1.9 fusion.32
  2285.4 4.8 convolution_subtract_fusion
  2290.2 1.9 fusion.30
  2292.1 6.8 fusion.6
  2298.9 1.9 fusion.29
  2302.2 3.8 maximum_bitcast_fusion
  2306.1 9.0 copy.180
  2315.1 4.5 gather_fusion.2
  2319.6 6.9 fusion.9
  2326.9 9.0 copy.177
  2335.9 8.4 select_select_fusion
  2344.3 9.0 copy.183
  2353.3 59.0 %all-reduce.7.cloned.1.call-done = f32[2048,512]{1,0:T(8,128)} async-done(((f32[2048,512]{1,0:T(8,128)}), f32[2048,512]{1,0:T(8,128)}) %all-reduce.7.cloned.1.call-update) | async-done | bytes 4194320 | tf_op jit(solution)/shard_map/psum | solution.py:16
  2412.3 62.3 %subtract_select_fusion = f32[4096,2048]{0,1:T(8,128)} fusion(f32[4096,2048]{0,1:T(8,128)} %add_add_fusion, pred[4096]{0:T(1024)(128)(4,1)S(1)} %fusion.46, pred[2048]{0:T(1024)(128)(4,1)S(1)} %fusion.52, f32[4096,512]{0,1:T(8,128)} %select_select_fusion, f32[2048,512]{1,0:T(8,128)} %all-reduce.7.cloned.1.call-done), kind=kOutput, calls=%fused_computation.11 | convolution fusion | flops 51564773376 | bytes 79697920 | tf_op jit(solution)/shard_map/rp,cp->rc/dot_general | solution.py:122
  2474.7 33.3 %copy.182 = f32[4096,2048]{1,0:T(8,128)} copy(f32[4096,2048]{0,1:T(8,128)} %subtract_select_fusion) | data formatting | bytes 67108864
  (140 shorter events, 21.9 us)
Async XLA Ops:
  58.2 190.7 %all-to-all-start = ((f32[2,2048,1024]{2,0,1:T(2,128)}), f32[2,2048,1024]{2,0,1:T(2,128)}, u32[]{:S(2)}, u32[]{:S(2)}) async-start(f32[2,2048,1024]{2,0,1:T(2,128)} %copy.167), calls=%async_computation | async-start | bytes 33554432 | tf_op jit(solution)/shard_map/all_to_all | solution.py:78
  384.0 7.1 copy-start.10
  384.0 7.4 copy-start.13
  384.0 369.6 %all-to-all-start.1 = ((f32[2,512,4096]{2,0,1:T(2,128)}), f32[2,512,4096]{2,0,1:T(2,128)}, u32[]{:S(2)}, u32[]{:S(2)}) async-start(f32[2,512,4096]{2,0,1:T(2,128)} %copy.170), calls=%async_computation.1 | async-start | bytes 33554432 | tf_op jit(solution)/shard_map/all_to_all | solution.py:82
  390.7 1685.4 %all-reduce.9.cloned.1.call-start = ((), (), s32[]{:S(2)}) async-start(), calls=%async_computation.3 | async-start | bytes 16777216 | tf_op jit(solution)/shard_map/psum | solution.py:16
  784.4 40.0 %copy-start.12 = (pred[2,32]{1,0:T(4,128)(4,1)S(1)}, pred[2,32]{1,0:T(4,128)(4,1)}, u32[]{:S(2)}) copy-start(pred[2,32]{1,0:T(4,128)(4,1)} %get-tuple-element.89) | copy-start | bytes 196
  950.1 190.8 %copy-start.9 = (f32[2,32]{0,1:T(8,128)S(1)}, f32[2,32]{0,1:T(8,128)}, u32[]{:S(2)}) copy-start(f32[2,32]{0,1:T(8,128)} %copy.172) | copy-start | bytes 772
  950.1 190.8 %copy-start.11 = (f32[2,64]{1,0:T(2,128)S(1)}, f32[2,64]{1,0:T(2,128)}, u32[]{:S(2)}) copy-start(f32[2,64]{1,0:T(2,128)} %fusion.28) | copy-start | bytes 1540
  950.1 190.8 %copy-start.14 = (pred[2,64]{1,0:T(4,128)(4,1)S(1)}, pred[2,64]{1,0:T(4,128)(4,1)}, u32[]{:S(2)}) copy-start(pred[2,64]{1,0:T(4,128)(4,1)} %compare_and_fusion.7) | copy-start | bytes 388
  1800.2 338.1 %all-reduce.11.cloned.1.call-start = ((), (), s32[]{:S(2)}) async-start(), calls=%async_computation.4 | async-start | bytes 4194304 | tf_op jit(solution)/shard_map/psum | solution.py:16
  2076.1 5.5 copy-start.8
  2076.1 5.6 copy-start.7
  2076.1 5.7 copy-start.6
  2076.1 5.7 copy-start.5
  2082.0 3.4 copy-start.3
  2086.8 325.5 %all-reduce.7.cloned.1.call-start = ((), (), s32[]{:S(2)}) async-start(), calls=%async_computation.2 | async-start | bytes 8388608 | tf_op jit(solution)/shard_map/psum | solution.py:16
  2236.1 40.2 %copy-start.4 = (f32[512,512]{1,0:T(8,128)}, f32[512,512]{1,0:T(8,128)S(1)}, u32[]{:S(2)}) copy-start(f32[512,512]{1,0:T(8,128)S(1)} %get-tuple-element.187) | copy-start | bytes 3145732
  2285.4 15.5 copy-start
  2292.1 8.7 copy-start.1
  2300.9 1.4 copy-start.2
Sparse Core Ops, SparseCore 0:
  1800.3 275.7 all-reduce.8
  2086.9 51.3 all-reduce.10
  2326.6 85.6 all-reduce.6
where the time goes:
time: 2540 us; the launch traced here: 2510 us
  local copies, waits for them, and re-layouts  1160 us (46%)
  waiting for transfers between devices  897 us (35%)
  other arithmetic  341 us (13%)
  matrix products  88.7 us (3%)
    slice x3, local copies, waits for them, and re-layouts, on_device(): extended = front_matrix + contributions[0] + contributions[1]  413 us
    psum x3, waiting for transfers between devices, spread_2(): return lax.psum(jnp.where(mine, shard, jnp.zeros_like(shard)), axis)  386 us
    all_to_all x1, waiting for transfers between devices, on_device(): lax.all_to_all(onward, 'col', split_axis=1, concat_axis=1, tiled=True)  329 us
    gather x3, local copies, waits for them, and re-layouts, place_blocks(): return jnp.take(picked, row_source, axis=1)  272 us
    all_to_all x1, waiting for transfers between devices, on_device(): lax.all_to_all(outgoing, 'row', split_axis=1, concat_axis=1, tiled=True)  182 us
    squeeze x2, local copies, waits for them, and re-layouts, on_device(): extended = front_matrix + contributions[0] + contributions[1]  109 us
    mul x1, other arithmetic, on_device(): placed * col_weight[:, :, None, None, None]  88.2 us
    unnamed x40, local copies, waits for them, and re-layouts  83.9 us
  transfers between devices with their start and end apart: 5, of which 5 were waited for; matrix products, arithmetic and copies ran while one was open for 2% of the time, Pallas kernels for 0%

commit v1 on v0

--- a/solution.py
+++ b/solution.py
@@ -9,20 +9,12 @@
 
 
 exact_mode = lax.Precision.HIGHEST
+split_mode = lax.Precision.HIGH
 
 
 def spread_2(shard, axis, root):
     mine = lax.axis_index(axis) == root
     return lax.psum(jnp.where(mine, shard, jnp.zeros_like(shard)), axis)
-
-
-def take_rows(source, indices):
-    return jnp.take(source, indices, axis=0)
-
-
-def place_blocks(arrived, col_source, row_source):
-    picked = jnp.take(arrived, col_source, axis=0)
-    return jnp.take(picked, row_source, axis=1)
 
 
 def on_device(front_matrix, child_schur, child_index, child_valid):
@@ -68,19 +60,21 @@
     local_bcol = col_place + col_count * jnp.arange(child_colblk)
     mine_colkey = jnp.take(col_key, local_bcol, axis=1)
     col_hit_send = mine_colkey[:, :, None] == jnp.arange(col_slots)[None, None, :]
-    src_col = jnp.sum(
-        col_hit_send.astype(jnp.int32) * jnp.arange(child_colblk)[None, :, None], axis=1
-    )
-    has_col = jnp.sum(col_hit_send.astype(jnp.float32), axis=1)
+    eye = jnp.eye(BLK, dtype=jnp.float32)
+    chunk = col_multi * BLK
+    sorter = col_hit_send.astype(jnp.float32)[:, :, None, :, None] * eye[None, None, :, None, :]
+    sorter = sorter.reshape(2, child_colblk * BLK, col_slots * BLK)
     blocks = child_schur.reshape(2, child_rowblk, BLK, child_colblk * BLK)
-    outgoing = jax.vmap(take_rows)(blocks, src_row)
-    outgoing = outgoing.reshape(2, row_slots * BLK, child_colblk * BLK)
-    section_one = lax.all_to_all(outgoing, "row", split_axis=1, concat_axis=1, tiled=True)
-    section_one = section_one.reshape(2, row_slots, BLK, child_colblk, BLK).transpose(0, 3, 1, 2, 4)
-    onward = jax.vmap(take_rows)(section_one, src_col) * has_col[:, :, None, None, None]
-    onward = onward.reshape(2, col_slots * row_slots, BLK * BLK)
-    section_two = lax.all_to_all(onward, "col", split_axis=1, concat_axis=1, tiled=True)
-    arrived = section_two.reshape(2, col_slots, row_slots, BLK, BLK)
+    arrived = []
+    for child in range(2):
+        outgoing = jnp.take(blocks[child], src_row[child], axis=0, mode="clip")
+        section_one = lax.all_to_all(outgoing, "row", split_axis=0, concat_axis=0, tiled=True)
+        onward = jnp.dot(
+            section_one.reshape(row_slots * BLK, child_colblk * BLK), sorter[child], precision=split_mode
+        )
+        onward = onward.reshape(row_slots * BLK, col_count, chunk).transpose(1, 0, 2)
+        section_two = lax.all_to_all(onward, "col", split_axis=0, concat_axis=0, tiled=True)
+        arrived.append(section_two.transpose(1, 0, 2).reshape(row_slots * BLK, col_slots * BLK))
     front_rowblk = row_place + row_count * jnp.arange(row_blocks)
     match_rows = (child_index[:, None, :] == front_rowblk[None, :, None]).astype(jnp.int32)
     row_slot_of = sender_row[None, :] * per_owner + row_rank
@@ -89,22 +83,29 @@
     front_colblk = col_place + col_count * jnp.arange(col_blocks)
     match_cols = (child_index[:, None, :] == front_colblk[None, :, None]).astype(jnp.int32)
     col_slot_of = sender_col[None, :] * col_multi + col_rank
-    col_source = jnp.sum(match_cols * col_slot_of[:, None, :], axis=2)
-    col_weight = jnp.sum(match_cols.astype(jnp.float32) * validity[:, None, :], axis=2)
-    placed = jax.vmap(place_blocks)(arrived, col_source, row_source)
-    placed = placed * col_weight[:, :, None, None, None] * row_weight[:, None, :, None, None]
-    contributions = placed.transpose(0, 2, 3, 1, 4).reshape(2, local_rows, local_cols)
-    extended = front_matrix + contributions[0] + contributions[1]
+    slot_hit = (col_slot_of[:, :, None] == jnp.arange(col_slots)[None, None, :]).astype(jnp.float32)
+    placer = jnp.einsum(
+        "kbs,kjb->ksj", slot_hit, match_cols.astype(jnp.float32) * validity[:, None, :], precision=exact_mode
+    )
+    placer = placer[:, :, None, :, None] * eye[None, None, :, None, :]
+    placer = placer.reshape(2, col_slots * BLK, local_cols)
+    extended = front_matrix.reshape(row_blocks, BLK, local_cols)
+    for child in range(2):
+        spread_cols = jnp.dot(arrived[child], placer[child], precision=split_mode)
+        spread_cols = spread_cols.reshape(row_slots, BLK, local_cols)
+        placed = jnp.take(spread_cols, row_source[child], axis=0, mode="clip")
+        extended = extended + placed * row_weight[child][:, None, None]
+    extended = extended.reshape(local_rows, local_cols)
     panel_width = PANEL // BLK
-    columns = []
-    for root_index in range(panel_width):
-        columns.append(spread_2(extended[:, :BLK], "col", root_index))
-    panel_cols = jnp.concatenate(columns, axis=1)
-    corner_rows = []
-    for root_index in range(panel_width):
-        start = root_index // row_count * BLK
-        corner_rows.append(spread_2(panel_cols[start : start + BLK], "row", root_index % row_count))
-    corner = jnp.concatenate(corner_rows, axis=0)
+    half = local_rows // 2
+    first = jnp.concatenate([extended[:half, :BLK], extended[half:, :BLK]], axis=1)
+    gathered = lax.all_gather(first, "col")[:panel_width]
+    panel_cols = gathered.reshape(panel_width, half, 2, BLK).transpose(2, 1, 0, 3)
+    panel_cols = panel_cols.reshape(local_rows, PANEL)
+    corner_count = panel_width // row_count
+    corner_rows = lax.all_gather(panel_cols[: corner_count * BLK], "row")
+    corner = corner_rows.reshape(row_count, corner_count, BLK, PANEL).transpose(1, 0, 2, 3)
+    corner = corner.reshape(PANEL, PANEL)
     lower_factor = jnp.linalg.cholesky(corner)
     solved = jax.scipy.linalg.solve_triangular(lower_factor, panel_cols.T, lower=True).T
     logical_blk = jnp.arange(row_blocks) * row_count + row_place
@@ -119,7 +120,7 @@
     chosen = lax.dynamic_index_in_dim(arranged, col_place // row_count, axis=1, keepdims=False)
     chosen = chosen.reshape(col_blocks * BLK, PANEL)
     across = spread_2(chosen, "row", col_place % row_count)
-    update = jnp.einsum("rp,cp->rc", panel_factor, across, precision=exact_mode)
+    update = jnp.einsum("rp,cp->rc", panel_factor, across, precision=split_mode)
     logical_row = jnp.arange(local_rows) // BLK * row_count + row_place
     logical_col = jnp.arange(local_cols) // BLK * col_count + col_place
     retained = (logical_row >= panel_width)[:, None] & (logical_col >= panel_width)[None, :]

time: 2540 us -> 1310 us (0.52)
  local copies, waits for them, and re-layouts: 1160 us -> 266 us
  waiting for transfers between devices: 897 us -> 596 us
  other arithmetic: 341 us -> 199 us
  matrix products: 88.7 us -> 191 us
    slice x3 -> x5, local copies, waits for them, and re-layouts: 413 us -> 41.3 us  [the longest x1 21.5 us: on_device(): spread_cols = jnp.dot(arrived[child], placer[child], precision=split_mode)]
    psum x3 -> x1, waiting for transfers between devices: 386 us -> 58.9 us  [spread_2(): return lax.psum(jnp.where(mine, shard, jnp.zeros_like(shard)), axis)]
    gather x10 -> x4, local copies, waits for them, and re-layouts: 379 us -> 54.1 us  [the longest x2 38.5 us: on_device(): placed = jnp.take(spread_cols, row_source[child], axis=0, mode='clip')]
    all_gather x0 -> x2, waiting for transfers between devices: none -> 138 us  [the longest x1 123 us: on_device(): gathered = lax.all_gather(first, 'col')[:panel_width]]
    all_to_all x2 -> x4, waiting for transfers between devices: 511 us -> 399 us  [the longest x2 256 us: on_device(): lax.all_to_all(onward, 'col', split_axis=0, concat_axis=0, tiled=True)]
    dot_general x1 -> x6, matrix products: 62.3 us -> 164 us  [the longest x2 65.4 us: on_device(): spread_cols = jnp.dot(arrived[child], placer[child], precision=split_mode)]
    reshape x3 -> x1, local copies, waits for them, and re-layouts: 88.8 us -> 0.33 us  [on_device(): corner = corner.reshape(PANEL, PANEL)]
    mul x3 -> x2, other arithmetic: 95.4 us -> 13.5 us  [the longest x1 11.6 us: on_device(): placer = placer[:, :, None, :, None] * eye[None, None, :, None, :]]
  transfers between devices with their start and end apart: 5 -> 7, of which waited for: 5 -> 7; matrix products, arithmetic and copies ran while one was open for 2% -> 14% of each run, Pallas kernels for 0% -> 0%
where the time goes in v1:
time: 1310 us; the launch traced here: 1300 us
  waiting for transfers between devices  596 us (45%)
  local copies, waits for them, and re-layouts  266 us (20%)
  other arithmetic  199 us (15%)
  matrix products  191 us (15%)
  starting transfers between devices  34 us (3%)
  between operations  17 us (1%)
    all_to_all x2, waiting for transfers between devices, on_device(): lax.all_to_all(onward, 'col', split_axis=0, concat_axis=0, tiled=True)  256 us
    all_to_all x2, waiting for transfers between devices, on_device(): lax.all_to_all(outgoing, 'row', split_axis=0, concat_axis=0, tiled=True)  144 us
    all_gather x1, waiting for transfers between devices, on_device(): gathered = lax.all_gather(first, 'col')[:panel_width]  123 us
    another operation x15, other arithmetic, on_device(): lower_factor = jnp.linalg.cholesky(corner)  79.3 us
    dot_general x2, matrix products, on_device(): spread_cols = jnp.dot(arrived[child], placer[child], precision=split_mode)  65.4 us
    dot_general x1, matrix products, on_device(): update = jnp.einsum('rp,cp->rc', panel_factor, across, precision=split_mode)  62.6 us
    psum x1, waiting for transfers between devices, spread_2(): return lax.psum(jnp.where(mine, shard, jnp.zeros_like(shard)), axis)  58.9 us
    add x1, other arithmetic, on_device(): extended = extended + placed * row_weight[child][:, None, None]  43.1 us
  transfers between devices with their start and end apart: 7, of which 7 were waited for; matrix products, arithmetic and copies ran while one was open for 14% of the time, Pallas kernels for 0%

profile of v1, /device:TPU:0, one launch (start us, length us, event | category | flops | bytes accessed | tf_op | source)
XLA Modules:
  0.0 1303.3 jit_solution(6624002112751829848)
XLA Ops:
  9.2 11.1 fusion.75
  20.2 7.7 gather_fusion.1
  27.9 5.6 all-to-all-start
  33.6 7.9 gather_fusion.4
  41.4 85.9 %all-to-all-done = f32[32,64,1024]{2,1,0:T(8,128)} async-done(((f32[32,64,1024]{2,1,0:T(8,128)}), f32[32,64,1024]{2,1,0:T(8,128)}, u32[]{:S(2)}, u32[]{:S(2)}) %all-to-all-start) | async-done | bytes 8388640 | tf_op jit(solution)/shard_map/all_to_all | solution.py:71
  127.3 5.6 all-to-all-start.2
  136.2 6.4 fusion.74
  142.6 7.6 squeeze.25
  150.2 18.1 %convolution_bitcast_fusion.1 = f32[8,2048,128]{2,1,0:T(8,128)} fusion(f32[2048,1024,1]{1,0,2:T(8,128)} %bitcast.5, f32[8,128,1024]{2,1,0:T(8,128)} %bitcast.166), kind=kOutput, calls=%fused_computation.28 | convolution fusion | flops 12884901888 | bytes 20971520 | tf_op jit(solution)/shard_map/dot_general | solution.py:72
  168.3 57.9 %all-to-all-done.2 = f32[32,64,1024]{2,1,0:T(8,128)} async-done(((f32[32,64,1024]{2,1,0:T(8,128)}), f32[32,64,1024]{2,1,0:T(8,128)}, u32[]{:S(2)}, u32[]{:S(2)}) %all-to-all-start.2) | async-done | bytes 8388640 | tf_op jit(solution)/shard_map/all_to_all | solution.py:71
  226.1 17.3 %all-to-all-start.1 = ((f32[8,2048,128]{2,1,0:T(8,128)}), f32[8,2048,128]{2,1,0:T(8,128)}, u32[]{:S(2)}, u32[]{:S(2)}) async-start(f32[8,2048,128]{2,1,0:T(8,128)} %convolution_bitcast_fusion.1), calls=%async_computation.1 | async-start | bytes 16777216 | tf_op jit(solution)/shard_map/all_to_all | solution.py:76
  243.4 7.6 squeeze.28
  251.0 18.1 %convolution_bitcast_fusion = f32[8,2048,128]{2,1,0:T(8,128)} fusion(f32[2048,1024,1]{1,0,2:T(8,128)} %bitcast.18, f32[8,128,1024]{2,1,0:T(8,128)} %bitcast.167), kind=kOutput, calls=%fused_computation.27 | convolution fusion | flops 12884901888 | bytes 20971520 | tf_op jit(solution)/shard_map/dot_general | solution.py:72
  269.2 157.2 %all-to-all-done.1 = f32[8,2048,128]{2,1,0:T(8,128)} async-done(((f32[8,2048,128]{2,1,0:T(8,128)}), f32[8,2048,128]{2,1,0:T(8,128)}, u32[]{:S(2)}, u32[]{:S(2)}) %all-to-all-start.1) | async-done | bytes 8388640 | tf_op jit(solution)/shard_map/all_to_all | solution.py:76
  426.3 4.9 all-to-all-start.3
  431.6 11.6 broadcast_multiply_fusion
  443.2 21.5 %fusion.73 = (f32[1,16,64,32,64]{4,3,2,1,0:T(8,128)}, f32[1,16,64,32,64]{4,3,2,1,0:T(8,128)}) fusion(f32[2,16,64,32,64]{4,3,2,1,0:T(8,128)} %broadcast_multiply_fusion), kind=kLoop, calls=%fused_computation.188 | loop fusion | bytes 33554432 | tf_op jit(solution)/shard_map/slice | solution.py:94
  464.6 14.8 %reshape.530 = f32[1024,2048,1]{1,0,2:T(8,128)} reshape(f32[1,16,64,32,64]{4,3,2,1,0:T(8,128)} %get-tuple-element.32) | data formatting | bytes 16777216 | tf_op jit(solution)/shard_map/squeeze | solution.py:94
  479.4 14.8 %reshape.532 = f32[1024,2048,1]{1,0,2:T(8,128)} reshape(f32[1,16,64,32,64]{4,3,2,1,0:T(8,128)} %get-tuple-element.33) | data formatting | bytes 16777216 | tf_op jit(solution)/shard_map/squeeze | solution.py:94
  495.0 10.7 copy.83
  505.7 9.2 dot_general.33
  514.9 98.4 %all-to-all-done.3 = f32[8,2048,128]{2,1,0:T(8,128)} async-done(((f32[8,2048,128]{2,1,0:T(8,128)}), f32[8,2048,128]{2,1,0:T(8,128)}, u32[]{:S(2)}, u32[]{:S(2)}) %all-to-all-start.3) | async-done | bytes 8388640 | tf_op jit(solution)/shard_map/all_to_all | solution.py:76
  613.3 10.7 copy.84
  624.0 9.3 dot_general.39
  633.3 32.6 %fusion.76 = f32[32,64,2048]{2,1,0:T(8,128)} fusion(f32[32,64,1024]{2,1,0:T(8,128)} %dot_general.33, f32[1024,2048,1]{1,0,2:T(8,128)} %reshape.530), kind=kOutput, calls=%fused_computation.191 | convolution fusion | flops 25769803776 | bytes 33554432 | tf_op jit(solution)/shard_map/dot_general | solution.py:94
  665.9 19.0 %gather_fusion.3 = f32[64,64,2048]{2,1,0:T(8,128)} fusion(f32[32,64,2048]{2,1,0:T(8,128)} %fusion.76, s32[1024]{0:T(1024)S(1)} %pad_clamp_fusion.3), kind=kCustom, calls=%fused_computation.3 | custom fusion | bytes 67109120 | tf_op jit(solution)/shard_map/jit(_take)/gather | solution.py:96
  685.0 32.8 %fusion.77 = f32[32,64,2048]{2,1,0:T(8,128)} fusion(f32[32,64,1024]{2,1,0:T(8,128)} %dot_general.39, f32[1024,2048,1]{1,0,2:T(8,128)} %reshape.532), kind=kOutput, calls=%fused_computation.192 | convolution fusion | flops 25769803776 | bytes 33554432 | tf_op jit(solution)/shard_map/dot_general | solution.py:94
  717.7 19.5 %gather_fusion.5 = f32[64,64,2048]{2,1,0:T(8,128)} fusion(f32[32,64,2048]{2,1,0:T(8,128)} %fusion.77, s32[1024]{0:T(1024)S(1)} %pad_clamp_fusion.1), kind=kCustom, calls=%fused_computation.5 | custom fusion | bytes 67109120 | tf_op jit(solution)/shard_map/jit(_take)/gather | solution.py:96
  737.2 43.1 %fusion = f32[4096,2048]{1,0:T(8,128)} fusion(f32[64,64,2048]{2,1,0:T(8,128)} %gather_fusion.5, f32[4096,2048]{1,0:T(8,128)} %param.4, f32[64,64,2048]{2,1,0:T(8,128)} %gather_fusion.3, f32[4096]{0:T(1024)S(1)} %mul.247, f32[4096]{0:T(1024)S(1)} %mul.242), kind=kLoop, calls=%fused_computation.10 | loop fusion | flops 33554432 | bytes 134250496 | tf_op jit(solution)/shard_map/add | solution.py:97
  783.4 123.3 %all-gather.5.cloned.1.call-done = f32[16384,128]{1,0:T(8,128)} async-done(((f32[2048,128]{1,0:T(8,128)}), f32[16384,128]{1,0:T(8,128)}) %all-gather.5.cloned.1.call-update) | async-done | bytes 8388624 | tf_op jit(solution)/shard_map/all_gather | solution.py:102
  906.8 9.1 copy.85
  915.9 9.9 copy.95
  925.8 7.8 copy.86
  933.6 8.1 copy.96
  941.8 3.4 copy-done.1
  946.8 14.3 %all-gather.7.cloned.1.call-done = f32[512,512]{0,1:T(8,128)} async-done(((f32[128,512]{0,1:T(8,128)}), f32[512,512]{0,1:T(8,128)}) %all-gather.7.cloned.1.call-update) | async-done | bytes 1048592 | tf_op jit(solution)/shard_map/all_gather | solution.py:106
  963.4 11.7 cholesky.104
  975.2 9.8 custom-call.31
  985.7 11.7 cholesky.217
  998.8 9.9 custom-call.32
  1009.4 11.7 cholesky.238
  1021.8 9.8 custom-call.33
  1032.2 11.9 cholesky.255
  1047.5 10.5 while.1
  1048.1 2.0 bitcast_dynamic-update-slice_fusion.2
  1050.7 2.0 bitcast_dynamic-update-slice_fusion.2
  1053.3 2.0 bitcast_dynamic-update-slice_fusion.2
  1055.9 2.0 bitcast_dynamic-update-slice_fusion.2
  1058.0 40.2 %custom-call.34 = f32[4,128,128]{1,2,0:T(8,128)S(1)} custom-call(f32[4,128,128]{2,1,0:T(8,128)} %get-tuple-element.9), custom_call_target="InvertDiagBlocksLowerTriangular" | custom-call | tf_op jit(solution)/shard_map/jit(_solve_triangular)/triangular_solve | solution.py:110
  1098.1 3.5 fusion.15
  1101.6 3.6 convolution_subtract_fusion.1
  1105.2 1.9 fusion.34
  1107.2 4.8 convolution_subtract_fusion
  1114.0 6.8 fusion.8
  1120.8 1.9 fusion.31
  1124.1 3.8 maximum_bitcast_fusion
  1127.9 8.9 copy.93
  1136.9 4.5 gather_fusion.6
  1141.4 6.9 fusion.11
  1148.6 9.0 copy.90
  1157.6 8.5 select_select_fusion
  1166.1 9.0 copy.94
  1175.1 58.9 %all-reduce.3.cloned.1.call-done = f32[2048,512]{1,0:T(8,128)} async-done(((f32[2048,512]{1,0:T(8,128)}), f32[2048,512]{1,0:T(8,128)}) %all-reduce.3.cloned.1.call-update) | async-done | bytes 4194320 | tf_op jit(solution)/shard_map/psum | solution.py:17
  1234.0 62.6 %subtract_select_fusion = f32[4096,2048]{1,0:T(8,128)} fusion(f32[4096,2048]{1,0:T(8,128)} %fusion, pred[2048]{0:T(1024)(128)(4,1)S(1)} %fusion.60, pred[4096]{0:T(1024)(128)(4,1)S(1)} %fusion.50, f32[4096,512]{0,1:T(8,128)} %select_select_fusion, f32[2048,512]{1,0:T(8,128)} %all-reduce.3.cloned.1.call-done), kind=kOutput, calls=%fused_computation.13 | convolution fusion | flops 25794969600 | bytes 79697920 | tf_op jit(solution)/shard_map/rp,cp->rc/dot_general | solution.py:123
  (116 shorter events, 23.9 us)
Async XLA Ops:
  27.9 99.4 %all-to-all-start = ((f32[32,64,1024]{2,1,0:T(8,128)}), f32[32,64,1024]{2,1,0:T(8,128)}, u32[]{:S(2)}, u32[]{:S(2)}) async-start(f32[32,64,1024]{2,1,0:T(8,128)} %gather_fusion.1), calls=%async_computation | async-start | bytes 16777216 | tf_op jit(solution)/shard_map/all_to_all | solution.py:71
  127.3 98.8 %all-to-all-start.2 = ((f32[32,64,1024]{2,1,0:T(8,128)}), f32[32,64,1024]{2,1,0:T(8,128)}, u32[]{:S(2)}, u32[]{:S(2)}) async-start(f32[32,64,1024]{2,1,0:T(8,128)} %gather_fusion.4), calls=%async_computation.2 | async-start | bytes 16777216 | tf_op jit(solution)/shard_map/all_to_all | solution.py:71
  226.1 200.2 %all-to-all-start.1 = ((f32[8,2048,128]{2,1,0:T(8,128)}), f32[8,2048,128]{2,1,0:T(8,128)}, u32[]{:S(2)}, u32[]{:S(2)}) async-start(f32[8,2048,128]{2,1,0:T(8,128)} %convolution_bitcast_fusion.1), calls=%async_computation.1 | async-start | bytes 16777216 | tf_op jit(solution)/shard_map/all_to_all | solution.py:76
  269.2 162.2 %copy-start.6 = (s32[2,128]{1,0:T(2,128)S(1)}, s32[2,128]{1,0:T(2,128)}, u32[]{:S(2)}) copy-start(s32[2,128]{1,0:T(2,128)} %param.7) | copy-start | bytes 3076
  269.2 162.2 %copy-start.5 = (s32[2,128]{1,0:T(2,128)S(1)}, s32[2,128]{1,0:T(2,128)}, u32[]{:S(2)}) copy-start(s32[2,128]{1,0:T(2,128)} %param.6) | copy-start | bytes 3076
  426.3 187.0 %all-to-all-start.3 = ((f32[8,2048,128]{2,1,0:T(8,128)}), f32[8,2048,128]{2,1,0:T(8,128)}, u32[]{:S(2)}, u32[]{:S(2)}) async-start(f32[8,2048,128]{2,1,0:T(8,128)} %convolution_bitcast_fusion), calls=%async_computation.3 | async-start | bytes 16777216 | tf_op jit(solution)/shard_map/all_to_all | solution.py:76
  431.3 475.5 %all-gather.5.cloned.1.call-start = ((), (), s32[]{:S(2)}) async-start(), calls=%async_computation.5 | async-start | bytes 9437184 | tf_op jit(solution)/shard_map/all_gather | solution.py:102
  783.4 177.7 %all-gather.7.cloned.1.call-start = ((), (), s32[]{:S(2)}) async-start(), calls=%async_computation.6 | async-start | bytes 1310720 | tf_op jit(solution)/shard_map/all_gather | solution.py:106
  941.7 3.4 copy-start.1
  945.9 288.1 %all-reduce.3.cloned.1.call-start = ((), (), s32[]{:S(2)}) async-start(), calls=%async_computation.4 | async-start | bytes 8388608 | tf_op jit(solution)/shard_map/psum | solution.py:17
  1058.0 40.2 %copy-start.4 = (f32[512,512]{1,0:T(8,128)}, f32[512,512]{1,0:T(8,128)S(1)}, u32[]{:S(2)}) copy-start(f32[512,512]{1,0:T(8,128)S(1)} %get-tuple-element.131) | copy-start | bytes 3145732
  1107.2 15.6 %copy-start = (f32[128,4096]{1,0:T(8,128)}, f32[128,4096]{1,0:T(8,128)S(1)}, u32[]{:S(2)}) copy-start(f32[128,4096]{1,0:T(8,128)S(1)} %fusion.34) | copy-start | bytes 6291460
  1114.0 8.8 copy-start.2
  1122.8 1.3 copy-start.3
Sparse Core Ops, SparseCore 0:
  783.5 123.2 all-gather.4
  946.0 15.0 all-gather.6
  1148.4 85.5 all-reduce.2
